TPU v7x, 512 devices: a whole 4x8x8 slice. The times are simulated.
512 devices in a mesh: leaf: 64 (over z_lo, x, y), head: 8 (over z_hi, core).
Axes of the slice: x: 4, y: 8, z: 8 (z_hi: 4, z_lo: 2; z = z_hi * 2 + z_lo), core: 2. Of those that a mesh axis runs over, the one named last changes fastest.
Arguments:
- queries: bfloat16 [8192, 64, 576], P('leaf', 'head'), may hold values from -40 to 40
- leaf_latent: bfloat16 [8192, 576], P('leaf'), may hold values from -4 to 4
- node_latent: bfloat16 [64, 96, 576], P('leaf', 'head'), may hold values from -4 to 4
- grad_out: bfloat16 [8192, 64, 512], P('leaf', 'head'), may hold values from -6 to 6
- leaf_nodes: int32 [128, 3], P('leaf'), may hold values from 0 to 63, as said below
- leaf_lengths: int32 [128], P('leaf'), may hold values from 1 to 64, 5120 in all
Outputs:
- attention: bfloat16 [8192, 64, 512], P('leaf', 'head')
- node_grad: bfloat16 [64, 96, 576], P('leaf', 'head')
- leaf_grad: bfloat16 [8192, 576], P('leaf')
Inputs may be any that keep to these rules, and one draw needn't show every extreme that they name: `leaf_nodes`: each row lists three different nodes: a root, one of its children and one of that child's children. Every node has one level and one parent; which nodes are used and how often varies.
All inputs are finite; a program needn't handle non-finite values. No bound on the sum of `leaf_lengths` on one device may be relied on, other than what follows from the above.
Results may differ from a plain program's by a relative error of at most 0.0095.
Values may be sent and summed in bfloat16 or wider, within the bound.
A program may use at most 64 MiB of HBM per device.

v0:
```python
import jax
import jax.numpy as jnp
from jax import lax
from jax.sharding import PartitionSpec as P

LAT = 512
NODE_ROWS = 96
score_scale = 192.0 ** (-0.5)


def from_everyone(shard, axis):
    devices = lax.axis_size(axis)
    return lax.all_to_all(
        jnp.broadcast_to(shard[None], (devices, *shard.shape)), axis, 0, 0, tiled=True
    )


def in_order(pieces, dim):
    pieces = jnp.moveaxis(pieces, 0, dim)
    lengths = pieces.shape
    return pieces.reshape(*lengths[:dim], lengths[dim] * lengths[dim + 1], *lengths[dim + 2 :])


def gather_directly(shard, axis, dim):
    pieces = from_everyone(shard, axis)
    return in_order(pieces, dim)


def cut_along(shard, dim, devices):
    before, after = (shard.shape[:dim], shard.shape[dim + 1 :])
    return jnp.moveaxis(shard.reshape(*before, devices, -1, *after), dim, 0)


def sum_at_owner(shard, axis, dim):
    pieces = cut_along(shard, dim, lax.axis_size(axis))
    arrived = lax.all_to_all(pieces, axis, split_axis=0, concat_axis=0, tiled=True)
    return arrived.astype(jnp.float32).sum(axis=0)


def body(queries, leaf_latent, node_latent, grad_out, leaf_nodes, leaf_lengths):
    rows, heads, width = queries.shape
    leaves = leaf_nodes.shape[0]
    leaf_rows = rows // leaves
    slices = gather_directly(node_latent, "leaf", 0)
    total_nodes = slices.shape[0]
    node_ids = leaf_nodes.reshape(-1)
    picker = (node_ids[:, None] == jnp.arange(total_nodes, dtype=jnp.int32)[None, :]).astype(
        jnp.bfloat16
    )
    chosen = jnp.dot(picker, slices.reshape(total_nodes, -1), preferred_element_type=jnp.float32)
    chosen = chosen.astype(jnp.bfloat16).reshape(leaves * 3, -1, width)
    whole_nodes = gather_directly(chosen, "head", 1)
    node_keys = whole_nodes.reshape(leaves, 3 * NODE_ROWS, width)
    keys = jnp.concatenate([node_keys, leaf_latent.reshape(leaves, leaf_rows, width)], axis=1)
    values = keys[:, :, :LAT]
    total_keys = keys.shape[1]
    query = queries.reshape(leaves, leaf_rows * heads, width)
    row_of = jnp.arange(leaf_rows * heads, dtype=jnp.int32) // heads
    key_index = jnp.arange(total_keys, dtype=jnp.int32)
    visible = (key_index[None, :] < 3 * NODE_ROWS) | (
        key_index[None, :] - 3 * NODE_ROWS <= row_of[:, None]
    )
    live = (row_of[None, :] < leaf_lengths[:, None]).astype(jnp.float32)[..., None]
    scores = (
        jnp.einsum("lqc,lkc->lqk", query, keys, preferred_element_type=jnp.float32) * score_scale
    )
    scores = jnp.where(visible[None], scores, -jnp.inf)
    top = jnp.max(scores, axis=-1, keepdims=True)
    expo = jnp.exp(scores - top)
    probs = expo / jnp.sum(expo, axis=-1, keepdims=True)
    probs_b = probs.astype(jnp.bfloat16)
    outputs = jnp.einsum("lqk,lkc->lqc", probs_b, values, preferred_element_type=jnp.float32)
    attention = (outputs * live).astype(jnp.bfloat16).reshape(rows, heads, LAT)
    masked_f = grad_out.reshape(leaves, leaf_rows * heads, LAT).astype(jnp.float32) * live
    masked = masked_f.astype(jnp.bfloat16)
    dprobs = jnp.einsum("lqc,lkc->lqk", masked, values, preferred_element_type=jnp.float32)
    delta = jnp.sum(masked_f * outputs, axis=-1)
    dscores = (score_scale * probs * (dprobs - delta[..., None])).astype(jnp.bfloat16)
    grad_keys = jnp.einsum("lqk,lqc->lkc", dscores, query, preferred_element_type=jnp.float32)
    grad_values = jnp.einsum("lqk,lqc->lkc", probs_b, masked, preferred_element_type=jnp.float32)
    grad_keys = jnp.concatenate(
        [grad_keys[:, :, :LAT] + grad_values, grad_keys[:, :, LAT:]], axis=2
    )
    node_terms = grad_keys[:, : 3 * NODE_ROWS].reshape(leaves * 3, NODE_ROWS, width)
    own_terms = grad_keys[:, 3 * NODE_ROWS :].reshape(rows, width)
    head_shares = sum_at_owner(node_terms.astype(jnp.bfloat16), "head", 1)
    owned = node_latent.shape[0]
    spread = jnp.dot(
        picker.T.astype(jnp.float32),
        head_shares.reshape(leaves * 3, -1),
        precision=lax.Precision.HIGHEST,
    )
    arrived = lax.all_to_all(
        spread.astype(jnp.bfloat16), "leaf", split_axis=0, concat_axis=0, tiled=True
    ).astype(spread.dtype)
    mine = jnp.sum(arrived.reshape(-1, owned, arrived.shape[1]), axis=0)
    node_grad = mine.reshape(node_latent.shape).astype(jnp.bfloat16)
    leaf_grad = lax.psum(own_terms, "head").astype(jnp.bfloat16)
    return (attention, node_grad, leaf_grad)


def solution(mesh):
    return jax.shard_map(
        body,
        mesh=mesh,
        in_specs=(
            P("leaf", "head", None),
            P("leaf", None),
            P("leaf", "head", None),
            P("leaf", "head", None),
            P("leaf", None),
            P("leaf"),
        ),
        out_specs=(P("leaf", "head", None), P("leaf", "head", None), P("leaf", None)),
        check_vma=False,
    )
```

profile of v0, /device:TPU:10, one launch (start us, length us, event | category | flops | bytes accessed | tf_op | source)
XLA Modules:
  0.0 189.7 jit_solution(587049199212427704)
XLA Ops:
  0.6 1.9 broadcast_in_dim.18
  2.5 12.5 %all-to-all-start = ((bf16[64,1,12,576]{3,2,1,0:T(8,128)(2,1)}), bf16[64,1,12,576]{3,2,1,0:T(8,128)(2,1)S(1)}, u32[]{:S(2)}, u32[]{:S(2)}) async-start(bf16[64,1,12,576]{3,2,1,0:T(8,128)(2,1)} %broadcast_in_dim.18), calls=%async_computation | async-start | bytes 2621440 | tf_op jit(solution)/shard_map/all_to_all | solution.py:13
  15.0 0.1 eq.15
  15.1 34.0 %all-to-all-done = bf16[64,1,12,576]{3,2,1,0:T(8,128)(2,1)S(1)} async-done(((bf16[64,1,12,576]{3,2,1,0:T(8,128)(2,1)}), bf16[64,1,12,576]{3,2,1,0:T(8,128)(2,1)S(1)}, u32[]{:S(2)}, u32[]{:S(2)}) %all-to-all-start) | async-done | bytes 884768 | tf_op jit(solution)/shard_map/all_to_all | solution.py:13
  49.1 0.9 reshape_reshape.6
  50.0 0.3 convolution_convert_fusion.1
  50.3 0.2 broadcast_in_dim.23
  50.5 0.0 copy-start.2
  50.5 1.0 broadcast_in_dim.24
  51.5 9.5 %all-to-all-start.1 = ((bf16[8,6,12,576]{3,2,1,0:T(8,128)(2,1)}), bf16[8,6,12,576]{3,2,1,0:T(8,128)(2,1)S(1)}, u32[]{:S(2)}, u32[]{:S(2)}) async-start(bf16[8,6,12,576]{3,2,1,0:T(8,128)(2,1)} %broadcast_in_dim.24), calls=%async_computation.1 | async-start | bytes 1966080 | tf_op jit(solution)/shard_map/all_to_all | solution.py:13
  61.1 0.2 copy.23
  61.2 0.0 copy-start.3
  61.2 0.9 copy.25
  62.1 2.0 %copy.26 = bf16[128,8,576]{2,1,0:T(8,128)(2,1)} copy(bf16[128,8,576]{0,2,1:T(8,128)(2,1)S(1)} %copy-done.1) | data formatting | bytes 2359296 | tf_op args[0]
  64.1 0.1 compare_convert_fusion
  64.2 0.9 compare_or_fusion
  65.1 24.2 %all-to-all-done.1 = bf16[8,6,12,576]{3,2,1,0:T(8,128)(2,1)S(1)} async-done(((bf16[8,6,12,576]{3,2,1,0:T(8,128)(2,1)}), bf16[8,6,12,576]{3,2,1,0:T(8,128)(2,1)S(1)}, u32[]{:S(2)}, u32[]{:S(2)}) %all-to-all-start.1) | async-done | bytes 663584 | tf_op jit(solution)/shard_map/all_to_all | solution.py:13
  89.3 0.1 copy.22
  89.4 0.4 reshape_reshape.7
  89.7 1.2 copy.24
  91.0 0.3 copy-done
  91.3 2.5 %fusion.9 = f32[2,512,352]{1,2,0:T(8,128)S(1)} fusion(bf16[2,512,576]{2,1,0:T(8,128)(2,1)S(1)} %bitcast.30, bf16[2,64,576]{1,2,0:T(8,128)(2,1)} %copy.25, bf16[2,288,576]{1,2,0:T(8,128)(2,1)} %copy.24, pred[512,352]{0,1:T(8,128)(4,1)} %compare_or_fusion), kind=kOutput, calls=%fused_computation.18 | convolution fusion | flops 417579008 | bytes 3612672 | tf_op jit(solution)/shard_map/lqc,lkc->lqk/dot_general | solution.py:65
  93.7 1.4 fusion.31
  95.1 2.2 %fusion.18 = f32[2,512,512]{2,1,0:T(8,128)S(1)} fusion(bf16[2,64,576]{1,2,0:T(8,128)(2,1)} %copy.25, bf16[2,288,576]{1,2,0:T(8,128)(2,1)} %copy.24, f32[2,512]{1,0:T(2,128)S(1)} %get-tuple-element.12, f32[2,512,352]{1,2,0:T(8,128)S(1)} %fusion.9), kind=kOutput, calls=%fused_computation.31 | convolution fusion | flops 371623264 | bytes 4354048 | tf_op jit(solution)/shard_map/lqk,lkc->lqc/dot_general | solution.py:72
  97.3 3.0 %fusion.4 = (f32[2,512]{1,0:T(2,128)S(1)}, bf16[2,512,512]{2,1,0:T(8,128)(2,1)}, bf16[2,512,512]{2,1,0:T(8,128)(2,1)}) fusion(f32[2,512,512]{2,1,0:T(8,128)S(1)} %fusion.18, f32[2,512]{1,0:T(2,128)S(1)} %compare_convert_fusion, bf16[2,512,512]{2,1,0:T(8,128)(2,1)} %bitcast.32), kind=kLoop, calls=%fused_computation.7 | loop fusion | flops 3668992 | bytes 5251072 | tf_op jit(solution)/shard_map/reduce_sum | solution.py:77
  100.4 5.2 %fusion.11 = f32[2,352,576]{1,2,0:T(8,128)} fusion(bf16[2,512,576]{2,1,0:T(8,128)(2,1)} %bitcast.29, bf16[2,512,512]{2,1,0:T(8,128)(2,1)} %get-tuple-element.11, f32[2,512]{1,0:T(2,128)S(1)} %get-tuple-element.9, f32[2,512,352]{1,2,0:T(8,128)} %get-tuple-element.13, f32[2,512]{1,0:T(2,128)S(1)} %get-tuple-element.12, bf16[2,64,576]{1,2,0:T(8,128)(2,1)} %copy.25, ...), kind=kOutput, calls=%fused_computation.20 | convolution fusion | flops 787578880 | bytes 6111232 | tf_op jit(solution)/shard_map/lqk,lqc->lkc/dot_general | solution.py:79
  105.5 2.5 %slice_add_fusion = f32[2,352,512]{1,2,0:T(8,128)S(1)} fusion(f32[2,352,576]{1,2,0:T(8,128)} %fusion.11, bf16[2,512,512]{2,1,0:T(8,128)(2,1)} %get-tuple-element.11, f32[2,512]{1,0:T(2,128)S(1)} %get-tuple-element.12, f32[2,512,352]{1,2,0:T(8,128)S(1)} %fusion.9), kind=kOutput, calls=%fused_computation.12 | convolution fusion | flops 370541920 | bytes 6819840 | tf_op jit(solution)/shard_map/lqk,lqc->lkc/dot_general | solution.py:80
  108.1 0.9 slice.22
  109.0 0.1 maximum_convert_fusion
  109.1 0.6 copy.32
  109.7 0.2 convert_element_type.66
  109.9 0.1 copy.33
  110.0 30.0 %all_to_all.24 = bf16[8,6,12,576]{3,2,1,0:T(8,128)(2,1)S(1)} all-to-all(bf16[8,6,12,576]{3,2,1,0:T(8,128)(2,1)S(1)} %copy.33), channel_id=1, replica_groups=mesh['leaf'=64,'head'=8] {'head'}, dimensions={0} | all-to-all | bytes 1327104 | tf_op jit(solution)/shard_map/all_to_all | solution.py:36
  140.0 0.2 convert_reduce_fusion
  140.2 0.1 reshape.165
  140.3 1.0 fusion.1
  141.3 0.5 broadcast.139
  141.8 1.3 reduce.2
  143.1 1.2 reshape.168
  144.2 6.5 %all-to-all-start.3 = ((bf16[64,2,3456]{2,1,0:T(2,128)(2,1)}), bf16[64,2,3456]{2,1,0:T(2,128)(2,1)S(1)}, u32[]{:S(2)}, u32[]{:S(2)}) async-start(bf16[64,2,3456]{2,1,0:T(2,128)(2,1)} %reshape.168), calls=%async_computation.3 | async-start | bytes 1769472 | tf_op jit(solution)/shard_map/all_to_all | solution.py:93
  150.8 0.2 pad_maximum_fusion.1
  151.0 0.2 copy.35
  151.2 34.6 %all-reduce.1 = bf16[128,576]{1,0:T(8,128)(2,1)S(1)} all-reduce(f32[128,576]{1,0:T(8,128)S(1)} %bitcast.31), channel_id=1, replica_groups=mesh['leaf'=64,'head'=8] {'head'}, use_global_device_ids=true, to_apply=%region_5.6 | all-reduce | flops 73728 | bytes 442368 | tf_op jit(solution)/shard_map/psum | solution.py:98
  185.8 0.8 copy.36
  186.6 0.0 all-to-all-done.3
  186.6 0.7 reshape.169
  187.3 1.7 reduce_sum.42
  189.0 0.7 convert_element_type.69
  (10 shorter events, 0.0 us)
Async XLA Ops:
  2.5 12.5 %copy-start.4 = (s32[2,3]{1,0:T(2,128)S(1)}, s32[2,3]{1,0:T(2,128)}, u32[]{:S(2)}) copy-start(s32[2,3]{1,0:T(2,128)} %param.10) | copy-start | bytes 76
  2.5 46.6 %all-to-all-start = ((bf16[64,1,12,576]{3,2,1,0:T(8,128)(2,1)}), bf16[64,1,12,576]{3,2,1,0:T(8,128)(2,1)S(1)}, u32[]{:S(2)}, u32[]{:S(2)}) async-start(bf16[64,1,12,576]{3,2,1,0:T(8,128)(2,1)} %broadcast_in_dim.18), calls=%async_computation | async-start | bytes 2621440 | tf_op jit(solution)/shard_map/all_to_all | solution.py:13
  50.5 10.6 %copy-start.2 = (bf16[128,576]{0,1:T(8,128)(2,1)S(1)}, bf16[128,576]{0,1:T(8,128)(2,1)}, u32[]{:S(2)}) copy-start(bf16[128,576]{0,1:T(8,128)(2,1)} %param.7) | copy-start | bytes 442372
  51.5 10.6 %copy-start.1 = (bf16[128,8,576]{0,2,1:T(8,128)(2,1)S(1)}, bf16[128,8,576]{0,2,1:T(8,128)(2,1)}, u32[]{:S(2)}) copy-start(bf16[128,8,576]{0,2,1:T(8,128)(2,1)} %param.6) | copy-start | bytes 3538948
  51.5 37.7 %all-to-all-start.1 = ((bf16[8,6,12,576]{3,2,1,0:T(8,128)(2,1)}), bf16[8,6,12,576]{3,2,1,0:T(8,128)(2,1)S(1)}, u32[]{:S(2)}, u32[]{:S(2)}) async-start(bf16[8,6,12,576]{3,2,1,0:T(8,128)(2,1)} %broadcast_in_dim.24), calls=%async_computation.1 | async-start | bytes 1966080 | tf_op jit(solution)/shard_map/all_to_all | solution.py:13
  61.2 2.9 %copy-start.3 = (s32[2]{0:T(128)S(1)}, s32[2]{0:T(128)}, u32[]{:S(2)}) copy-start(s32[2]{0:T(128)} %param.11) | copy-start | bytes 28
  89.7 1.5 copy-start
  144.2 42.4 %all-to-all-start.3 = ((bf16[64,2,3456]{2,1,0:T(2,128)(2,1)}), bf16[64,2,3456]{2,1,0:T(2,128)(2,1)S(1)}, u32[]{:S(2)}, u32[]{:S(2)}) async-start(bf16[64,2,3456]{2,1,0:T(2,128)(2,1)} %reshape.168), calls=%async_computation.3 | async-start | bytes 1769472 | tf_op jit(solution)/shard_map/all_to_all | solution.py:93
where the time goes:
time: 190 us
  blocking collectives  64.6 us (34%)
  waiting for transfers between devices  58.2 us (31%)
  starting transfers between devices  28.6 us (15%)
  local copies, waits for them, and re-layouts  15.1 us (8%)
  matrix products  13.6 us (7%)
  other arithmetic  8.84 us (5%)
    all_to_all x2, waiting for transfers between devices, from_everyone(): lax.all_to_all(jnp.broadcast_to(shard[None], (devices, *shard.shape)), ax...  58.2 us
    psum x1, blocking collectives, body(): leaf_grad = lax.psum(own_terms, 'head').astype(jnp.bfloat16)  34.6 us
    all_to_all x1, blocking collectives, sum_at_owner(): lax.all_to_all(pieces, axis, split_axis=0, concat_axis=0, tiled=True)  30 us
    all_to_all x2, starting transfers between devices, from_everyone(): lax.all_to_all(jnp.broadcast_to(shard[None], (devices, *shard.shape)), ax...  22 us
    all_to_all x1, starting transfers between devices, body(): lax.all_to_all(spread.astype(jnp.bfloat16), 'leaf', split_axis=0, concat_...  6.53 us
    dot_general x1, matrix products, body(): jnp.einsum('lqk,lqc->lkc', dscores, query, preferred_element_type=jnp.flo...  5.17 us
    unnamed x15, local copies, waits for them, and re-layouts  5.13 us
  transfers between devices with their start and end apart: 3, of which 2 were waited for; matrix products, arithmetic and copies ran while one was open for 3% of the time, Pallas kernels for 0%

commit v1 on v0

--- a/solution.py
+++ b/solution.py
@@ -95,7 +95,7 @@
     ).astype(spread.dtype)
     mine = jnp.sum(arrived.reshape(-1, owned, arrived.shape[1]), axis=0)
     node_grad = mine.reshape(node_latent.shape).astype(jnp.bfloat16)
-    leaf_grad = lax.psum(own_terms, "head").astype(jnp.bfloat16)
+    leaf_grad = jnp.sum(lax.all_gather(own_terms, "head"), axis=0).astype(jnp.bfloat16)
     return (attention, node_grad, leaf_grad)
 
 

time: 190 us -> 209 us (1.10)
  the two profiles are of different devices: /device:TPU:10 before, /device:TPU:8 now
where the time goes in v1:
time: 209 us; the launch traced here: 208 us
  blocking collectives  73.3 us (35%)
  waiting for transfers between devices  59 us (28%)
  starting transfers between devices  22.1 us (11%)
  local copies, waits for them, and re-layouts  15.2 us (7%)
  between operations  14.2 us (7%)
  matrix products  13.6 us (7%)
  other arithmetic  10.6 us (5%)
    all_to_all x2, waiting for transfers between devices, from_everyone(): lax.all_to_all(jnp.broadcast_to(shard[None], (devices, *shard.shape)), ax...  59 us
    all_to_all x1, blocking collectives, sum_at_owner(): lax.all_to_all(pieces, axis, split_axis=0, concat_axis=0, tiled=True)  44 us
    all_to_all x1, blocking collectives, body(): lax.all_to_all(spread.astype(jnp.bfloat16), 'leaf', split_axis=0, concat_...  29.3 us
    all_to_all x2, starting transfers between devices, from_everyone(): lax.all_to_all(jnp.broadcast_to(shard[None], (devices, *shard.shape)), ax...  22 us
    dot_general x1, matrix products, body(): jnp.einsum('lqk,lqc->lkc', dscores, query, preferred_element_type=jnp.flo...  5.17 us
    unnamed x16, local copies, waits for them, and re-layouts  4.37 us
  transfers between devices with their start and end apart: 3, of which 2 were waited for; matrix products, arithmetic and copies ran while one was open for 5% of the time, Pallas kernels for 0%

profile of v1, /device:TPU:8, one launch (start us, length us, event | category | flops | bytes accessed | tf_op | source)
XLA Modules:
  0.0 208.0 jit_solution(925171569472437312)
XLA Ops:
  7.2 1.9 broadcast_in_dim.18
  9.1 12.5 %all-to-all-start = ((bf16[64,1,12,576]{3,2,1,0:T(8,128)(2,1)}), bf16[64,1,12,576]{3,2,1,0:T(8,128)(2,1)S(1)}, u32[]{:S(2)}, u32[]{:S(2)}) async-start(bf16[64,1,12,576]{3,2,1,0:T(8,128)(2,1)} %broadcast_in_dim.18), calls=%async_computation | async-start | bytes 2621440 | tf_op jit(solution)/shard_map/all_to_all | solution.py:13
  21.6 0.1 eq.15
  21.7 34.9 %all-to-all-done = bf16[64,1,12,576]{3,2,1,0:T(8,128)(2,1)S(1)} async-done(((bf16[64,1,12,576]{3,2,1,0:T(8,128)(2,1)}), bf16[64,1,12,576]{3,2,1,0:T(8,128)(2,1)S(1)}, u32[]{:S(2)}, u32[]{:S(2)}) %all-to-all-start) | async-done | bytes 884768 | tf_op jit(solution)/shard_map/all_to_all | solution.py:13
  56.5 0.9 reshape_reshape.6
  57.5 0.3 convolution_convert_fusion.1
  57.7 0.2 broadcast_in_dim.23
  57.9 1.0 broadcast_in_dim.24
  58.9 9.5 %all-to-all-start.1 = ((bf16[8,6,12,576]{3,2,1,0:T(8,128)(2,1)}), bf16[8,6,12,576]{3,2,1,0:T(8,128)(2,1)S(1)}, u32[]{:S(2)}, u32[]{:S(2)}) async-start(bf16[8,6,12,576]{3,2,1,0:T(8,128)(2,1)} %broadcast_in_dim.24), calls=%async_computation.1 | async-start | bytes 1966080 | tf_op jit(solution)/shard_map/all_to_all | solution.py:13
  68.5 0.0 all-gather.2.cloned.1.call-start
  68.5 0.2 copy.22
  68.7 0.9 copy.24
  69.6 2.0 copy.25
  71.6 0.1 compare_convert_fusion
  71.7 0.9 compare_or_fusion
  72.5 24.1 %all-to-all-done.1 = bf16[8,6,12,576]{3,2,1,0:T(8,128)(2,1)S(1)} async-done(((bf16[8,6,12,576]{3,2,1,0:T(8,128)(2,1)}), bf16[8,6,12,576]{3,2,1,0:T(8,128)(2,1)S(1)}, u32[]{:S(2)}, u32[]{:S(2)}) %all-to-all-start.1) | async-done | bytes 663584 | tf_op jit(solution)/shard_map/all_to_all | solution.py:13
  96.7 0.1 copy.21
  96.8 0.4 reshape_reshape.7
  97.2 1.2 copy.23
  98.4 0.3 copy-done
  98.7 2.5 %fusion.9 = f32[2,512,352]{1,2,0:T(8,128)S(1)} fusion(bf16[2,512,576]{2,1,0:T(8,128)(2,1)S(1)} %bitcast.31, bf16[2,64,576]{1,2,0:T(8,128)(2,1)} %copy.24, bf16[2,288,576]{1,2,0:T(8,128)(2,1)} %copy.23, pred[512,352]{0,1:T(8,128)(4,1)} %compare_or_fusion), kind=kOutput, calls=%fused_computation.18 | convolution fusion | flops 417579008 | bytes 3612672 | tf_op jit(solution)/shard_map/lqc,lkc->lqk/dot_general | solution.py:65
  101.1 1.4 fusion.31
  102.5 2.2 %fusion.18 = f32[2,512,512]{2,1,0:T(8,128)S(1)} fusion(bf16[2,64,576]{1,2,0:T(8,128)(2,1)} %copy.24, bf16[2,288,576]{1,2,0:T(8,128)(2,1)} %copy.23, f32[2,512]{1,0:T(2,128)S(1)} %get-tuple-element.9, f32[2,512,352]{1,2,0:T(8,128)S(1)} %fusion.9), kind=kOutput, calls=%fused_computation.31 | convolution fusion | flops 371623264 | bytes 4354048 | tf_op jit(solution)/shard_map/lqk,lkc->lqc/dot_general | solution.py:72
  104.7 3.0 %fusion.4 = (f32[2,512]{1,0:T(2,128)S(1)}, bf16[2,512,512]{2,1,0:T(8,128)(2,1)}, bf16[2,512,512]{2,1,0:T(8,128)(2,1)}) fusion(f32[2,512,512]{2,1,0:T(8,128)S(1)} %fusion.18, f32[2,512]{1,0:T(2,128)S(1)} %compare_convert_fusion, bf16[2,512,512]{2,1,0:T(8,128)(2,1)} %bitcast.32), kind=kLoop, calls=%fused_computation.7 | loop fusion | flops 3668992 | bytes 5251072 | tf_op jit(solution)/shard_map/reduce_sum | solution.py:77
  107.8 5.2 %fusion.11 = f32[2,352,576]{1,2,0:T(8,128)} fusion(bf16[2,512,576]{2,1,0:T(8,128)(2,1)} %bitcast.30, bf16[2,512,512]{2,1,0:T(8,128)(2,1)} %get-tuple-element.8, f32[2,512]{1,0:T(2,128)S(1)} %get-tuple-element.6, f32[2,512,352]{1,2,0:T(8,128)} %get-tuple-element.10, f32[2,512]{1,0:T(2,128)S(1)} %get-tuple-element.9, bf16[2,64,576]{1,2,0:T(8,128)(2,1)} %copy.24, ...), kind=kOutput, calls=%fused_computation.20 | convolution fusion | flops 787578880 | bytes 6111232 | tf_op jit(solution)/shard_map/lqk,lqc->lkc/dot_general | solution.py:79
  112.9 2.5 %slice_add_fusion = f32[2,352,512]{1,2,0:T(8,128)S(1)} fusion(f32[2,352,576]{1,2,0:T(8,128)} %fusion.11, bf16[2,512,512]{2,1,0:T(8,128)(2,1)} %get-tuple-element.8, f32[2,512]{1,0:T(2,128)S(1)} %get-tuple-element.9, f32[2,512,352]{1,2,0:T(8,128)S(1)} %fusion.9), kind=kOutput, calls=%fused_computation.12 | convolution fusion | flops 370541920 | bytes 6819840 | tf_op jit(solution)/shard_map/lqk,lqc->lkc/dot_general | solution.py:80
  115.5 0.9 slice.22
  116.4 0.2 pad_maximum_fusion.1
  116.6 0.2 copy.34
  116.9 0.9 copy.35
  117.7 0.1 maximum_convert_fusion
  117.9 0.6 copy.31
  118.4 0.2 convert_element_type.66
  118.6 0.1 copy.32
  118.7 44.0 %all_to_all.24 = bf16[8,6,12,576]{3,2,1,0:T(8,128)(2,1)S(1)} all-to-all(bf16[8,6,12,576]{3,2,1,0:T(8,128)(2,1)S(1)} %copy.32), channel_id=1, replica_groups=mesh['leaf'=64,'head'=8] {'head'}, dimensions={0} | all-to-all | bytes 1327104 | tf_op jit(solution)/shard_map/all_to_all | solution.py:36
  162.7 0.2 convert_reduce_fusion
  162.9 0.1 reshape.162
  163.0 1.0 fusion.1
  164.0 0.5 broadcast.139
  164.5 1.3 reduce.2
  165.7 0.2 reshape.164
  166.0 29.3 %all_to_all.25 = bf16[64,2,3456]{2,1,0:T(2,128)(2,1)S(1)} all-to-all(bf16[64,2,3456]{2,1,0:T(2,128)(2,1)S(1)} %reshape.164), channel_id=1, replica_groups=mesh['leaf'=64,'head'=8] {'leaf'}, dimensions={0} | all-to-all | bytes 1769472 | tf_op jit(solution)/shard_map/all_to_all | solution.py:93
  195.3 0.7 reshape.165
  196.0 1.7 reduce_sum.51
  197.7 0.7 convert_element_type.69
  198.4 1.8 reduce_sum.52
  200.2 0.2 copy.43
  200.4 0.8 copy.37
  (14 shorter events, 0.1 us)
Async XLA Ops:
  9.1 12.5 %copy-start.4 = (s32[2,3]{1,0:T(2,128)S(1)}, s32[2,3]{1,0:T(2,128)}, u32[]{:S(2)}) copy-start(s32[2,3]{1,0:T(2,128)} %param.10) | copy-start | bytes 76
  9.1 47.5 %all-to-all-start = ((bf16[64,1,12,576]{3,2,1,0:T(8,128)(2,1)}), bf16[64,1,12,576]{3,2,1,0:T(8,128)(2,1)S(1)}, u32[]{:S(2)}, u32[]{:S(2)}) async-start(bf16[64,1,12,576]{3,2,1,0:T(8,128)(2,1)} %broadcast_in_dim.18), calls=%async_computation | async-start | bytes 2621440 | tf_op jit(solution)/shard_map/all_to_all | solution.py:13
  57.9 10.6 %copy-start.2 = (bf16[128,576]{0,1:T(8,128)(2,1)S(1)}, bf16[128,576]{0,1:T(8,128)(2,1)}, u32[]{:S(2)}) copy-start(bf16[128,576]{0,1:T(8,128)(2,1)} %param.7) | copy-start | bytes 442372
  58.9 10.6 %copy-start.1 = (bf16[128,8,576]{0,2,1:T(8,128)(2,1)S(1)}, bf16[128,8,576]{0,2,1:T(8,128)(2,1)}, u32[]{:S(2)}) copy-start(bf16[128,8,576]{0,2,1:T(8,128)(2,1)} %param.6) | copy-start | bytes 3538948
  58.9 37.7 %all-to-all-start.1 = ((bf16[8,6,12,576]{3,2,1,0:T(8,128)(2,1)}), bf16[8,6,12,576]{3,2,1,0:T(8,128)(2,1)S(1)}, u32[]{:S(2)}, u32[]{:S(2)}) async-start(bf16[8,6,12,576]{3,2,1,0:T(8,128)(2,1)} %broadcast_in_dim.24), calls=%async_computation.1 | async-start | bytes 1966080 | tf_op jit(solution)/shard_map/all_to_all | solution.py:13
  68.5 129.9 %all-gather.2.cloned.1.call-start = ((), (), s32[]{:S(2)}) async-start(), calls=%async_computation.4 | async-start | bytes 2654208 | tf_op jit(solution)/shard_map/all_gather | solution.py:98
  68.7 2.9 %copy-start.3 = (s32[2]{0:T(128)S(1)}, s32[2]{0:T(128)}, u32[]{:S(2)}) copy-start(s32[2]{0:T(128)} %param.11) | copy-start | bytes 28
  97.1 1.5 copy-start
Sparse Core Ops, SparseCore 0:
  117.9 50.2 all-gather.1
